TPU v7x, 32 devices: a whole 2x2x4 slice. The times are simulated.
32 devices in a mesh: group: 2 (over y), latent: 8 (over z, x), dp: 2 (over core).
Axes of the slice: x: 2, y: 2, z: 4, core: 2. Of those that a mesh axis runs over, the one named last changes fastest.
Arguments:
- tokens: bfloat16 [128, 4096], P(('group', 'latent', 'dp')), parts along dimension 0, may hold values from -6 to 6
- enc_weight: bfloat16 [8192, 1024], P('group', 'latent'), parts along dimension 0, may hold values from -0.09375 to 0.09375
- enc_bias: float32 [2048], P(('group', 'latent')), parts along dimension 0, may hold values from -1 to 0.25
- dec_weight: bfloat16 [2048, 4096], P(('group', 'latent')), parts along dimension 0, may hold values from -0.1875 to 0.1875
- dec_bias: float32 [8192], P('group'), parts along dimension 0, may hold values from -3 to 3
Outputs:
- reconstruction: float32 [128, 4096], P(('group', 'latent', 'dp')), parts along dimension 0
- new_enc_weight: bfloat16 [8192, 1024], P('group', 'latent'), parts along dimension 0
- new_enc_bias: float32 [2048], P(('group', 'latent')), parts along dimension 0
- new_dec_weight: bfloat16 [2048, 4096], P(('group', 'latent')), parts along dimension 0
- new_dec_bias: float32 [8192], P('group'), parts along dimension 0
There are 2 independent parts, one for each index of `group`. A program takes and returns all parts, laid end to end along the dimension named above; each array names one. Nothing has to cross between parts.
All inputs are finite; a program needn't handle non-finite values.
Results may differ from a plain program's by a relative error of at most 0.012.
The roundings to bfloat16 on the way count: a program that leaves them out, or rounds other values in their place, can miss the bound.
Values may be sent and summed in bfloat16 or wider, within the bound.
A program may use at most 64 MiB of HBM per device.

v0:
```python
import jax
import jax.numpy as jnp
from jax import lax
from jax.sharding import PartitionSpec as P

STEP_RATE = 0.1


def from_behind(block, axis, distance):
    devices = range(lax.axis_size(axis))
    route = [((i - distance) % len(devices), i) for i in devices]
    return lax.ppermute(block, axis, route)


def on_device(tokens, enc_weight, enc_bias, dec_weight, dec_bias):
    cycle_len = lax.axis_size("latent")
    slab_count = lax.axis_size("dp")
    cycle_pos = lax.axis_index("latent")
    tok_rows = tokens.shape[0]
    total_tokens = tok_rows * cycle_len * slab_count
    tokens_wide = tokens.astype(jnp.float32)
    centered = (tokens_wide - dec_bias).astype(jnp.bfloat16)
    gathered = lax.all_gather(centered, "latent", axis=0, tiled=True)
    preacts = jnp.dot(gathered, enc_weight, preferred_element_type=jnp.float32) + enc_bias
    latent_codes = jnp.maximum(preacts, 0.0).astype(jnp.bfloat16)
    partial_value = jnp.dot(latent_codes, dec_weight, preferred_element_type=jnp.float32)

    def pick(offset):
        start = offset % cycle_len * tok_rows
        return lax.dynamic_slice_in_dim(partial_value, start, tok_rows, 0)

    def advance(step_idx, carried):
        return from_behind(carried.astype(jnp.bfloat16), "latent", 1).astype(carried.dtype) + pick(
            cycle_pos - step_idx - 1
        )

    summed = lax.fori_loop(1, cycle_len, advance, pick(cycle_pos - 1))
    reconstruction = summed + dec_bias
    recon_error = (reconstruction - tokens_wide).astype(jnp.bfloat16)
    errors = lax.all_gather(recon_error, "latent", axis=0, tiled=True)
    back = lax.dot_general(
        errors, dec_weight, (((1,), (1,)), ((), ())), preferred_element_type=jnp.float32
    )
    code_grad = jnp.where(latent_codes > 0, back, 0.0).astype(jnp.bfloat16)
    grad_enc = lax.dot_general(
        gathered, code_grad, (((0,), (0,)), ((), ())), preferred_element_type=jnp.float32
    )
    grad_dec_cols = lax.dot_general(
        errors, latent_codes, (((0,), (0,)), ((), ())), preferred_element_type=jnp.float32
    )
    column_rates = jnp.sum(code_grad.astype(jnp.float32), axis=0)
    bias_term = jnp.sum(recon_error.astype(jnp.float32), axis=0) - jnp.dot(
        enc_weight.astype(jnp.float32), column_rates, precision=lax.Precision.HIGHEST
    )
    grad_dec_bias = lax.psum(bias_term, ("latent", "dp"))
    factor = STEP_RATE * 2.0 / total_tokens
    summed_enc, summed_dec, grad_enc_bias = (
        lax.psum(grad_enc.astype(jnp.bfloat16), "dp").astype(jnp.float32),
        lax.psum(grad_dec_cols.astype(jnp.bfloat16), "dp").astype(jnp.float32),
        lax.psum(column_rates.astype(jnp.bfloat16), "dp").astype(jnp.float32),
    )
    new_enc_weight = (enc_weight.astype(jnp.float32) - factor * summed_enc).astype(jnp.bfloat16)
    new_dec_weight = (dec_weight.astype(jnp.float32) - factor * summed_dec.T).astype(jnp.bfloat16)
    new_enc_bias = enc_bias - factor * grad_enc_bias
    new_dec_bias = dec_bias - factor * grad_dec_bias
    return (reconstruction, new_enc_weight, new_enc_bias, new_dec_weight, new_dec_bias)


def solution(mesh):
    return jax.shard_map(
        on_device,
        mesh=mesh,
        in_specs=(
            P(("group", "latent", "dp"), None),
            P("group", "latent"),
            P(("group", "latent")),
            P(("group", "latent"), None),
            P("group"),
        ),
        out_specs=(
            P(("group", "latent", "dp"), None),
            P("group", "latent"),
            P(("group", "latent")),
            P(("group", "latent"), None),
            P("group"),
        ),
        check_vma=False,
    )
```

profile of v0, /device:TPU:0, one launch (start us, length us, event | category | flops | bytes accessed | tf_op | source)
XLA Modules:
  0.0 198.7 jit_solution(11809243143569353338)
XLA Ops:
  7.2 0.8 fusion.6
  8.0 32.7 %all-gather = bf16[8,4,4096]{2,1,0:T(4,128)(2,1)S(1)} all-gather(bf16[1,4,4096]{2,1,0:T(4,128)(2,1)S(1)} %fusion.6), channel_id=1, replica_groups=mesh['group'=2,'latent'=8,'dp'=2] {'latent'}, dimensions={0}, use_global_device_ids=true | all-gather | bytes 294912 | tf_op jit(solution)/shard_map/all_gather | solution.py:23
  40.8 1.5 fusion.2
  42.6 47.2 %while.15 = (s32[]{:T(128)}, f32[4,4096]{1,0:T(4,128)S(1)}, s32[]{:T(128)}, f32[32,4096]{1,0:T(8,128)S(1)}, s32[]{:T(128)}, /*index=5*/s32[]{:T(128)}, s32[]{:T(...) while((s32[]{:T(128)}, f32[4,4096]{1,0:T(4,128)S(1)}, s32[]{:T(128)}, f32[32,4096]{1,0:T(8,128)S(1)}, ...), condition=%wide.region_1.2_spmd, body=%wide.region_0.1_spmd.sunk | while | flops 49171 | bytes 393548 | solution.py:37
  42.7 1.6 collective-permute-start
  44.3 5.1 %collective-permute-done = bf16[4,4096]{1,0:T(4,128)(2,1)S(1)} collective-permute-done((bf16[4,4096]{1,0:T(4,128)(2,1)S(1)}, bf16[4,4096]{1,0:T(4,128)(2,1)S(1)}, u32[]{:S(2)}, u32[]{:S(2)}) %collective-permute-start) | collective-permute-done | bytes 32800 | tf_op jit(solution)/shard_map/while/body/eval_jaxpr/ppermute | solution.py:12
  49.5 6.6 %collective-permute-done = bf16[4,4096]{1,0:T(4,128)(2,1)S(1)} collective-permute-done((bf16[4,4096]{1,0:T(4,128)(2,1)S(1)}, bf16[4,4096]{1,0:T(4,128)(2,1)S(1)}, u32[]{:S(2)}, u32[]{:S(2)}) %collective-permute-start) | collective-permute-done | bytes 32800 | tf_op jit(solution)/shard_map/while/body/eval_jaxpr/ppermute | solution.py:12
  56.2 6.6 %collective-permute-done = bf16[4,4096]{1,0:T(4,128)(2,1)S(1)} collective-permute-done((bf16[4,4096]{1,0:T(4,128)(2,1)S(1)}, bf16[4,4096]{1,0:T(4,128)(2,1)S(1)}, u32[]{:S(2)}, u32[]{:S(2)}) %collective-permute-start) | collective-permute-done | bytes 32800 | tf_op jit(solution)/shard_map/while/body/eval_jaxpr/ppermute | solution.py:12
  62.9 6.6 %collective-permute-done = bf16[4,4096]{1,0:T(4,128)(2,1)S(1)} collective-permute-done((bf16[4,4096]{1,0:T(4,128)(2,1)S(1)}, bf16[4,4096]{1,0:T(4,128)(2,1)S(1)}, u32[]{:S(2)}, u32[]{:S(2)}) %collective-permute-start) | collective-permute-done | bytes 32800 | tf_op jit(solution)/shard_map/while/body/eval_jaxpr/ppermute | solution.py:12
  69.7 6.6 %collective-permute-done = bf16[4,4096]{1,0:T(4,128)(2,1)S(1)} collective-permute-done((bf16[4,4096]{1,0:T(4,128)(2,1)S(1)}, bf16[4,4096]{1,0:T(4,128)(2,1)S(1)}, u32[]{:S(2)}, u32[]{:S(2)}) %collective-permute-start) | collective-permute-done | bytes 32800 | tf_op jit(solution)/shard_map/while/body/eval_jaxpr/ppermute | solution.py:12
  76.4 6.7 %collective-permute-done = bf16[4,4096]{1,0:T(4,128)(2,1)S(1)} collective-permute-done((bf16[4,4096]{1,0:T(4,128)(2,1)S(1)}, bf16[4,4096]{1,0:T(4,128)(2,1)S(1)}, u32[]{:S(2)}, u32[]{:S(2)}) %collective-permute-start) | collective-permute-done | bytes 32800 | tf_op jit(solution)/shard_map/while/body/eval_jaxpr/ppermute | solution.py:12
  83.3 6.6 %collective-permute-done = bf16[4,4096]{1,0:T(4,128)(2,1)S(1)} collective-permute-done((bf16[4,4096]{1,0:T(4,128)(2,1)S(1)}, bf16[4,4096]{1,0:T(4,128)(2,1)S(1)}, u32[]{:S(2)}, u32[]{:S(2)}) %collective-permute-start) | collective-permute-done | bytes 32800 | tf_op jit(solution)/shard_map/while/body/eval_jaxpr/ppermute | solution.py:12
  90.0 30.7 %all-gather.1 = bf16[8,4,4096]{2,1,0:T(4,128)(2,1)S(1)} all-gather(bf16[1,4,4096]{2,1,0:T(4,128)(2,1)S(1)} %fusion.9), channel_id=1, replica_groups=mesh['group'=2,'latent'=8,'dp'=2] {'latent'}, dimensions={0}, use_global_device_ids=true | all-gather | bytes 294912 | tf_op jit(solution)/shard_map/all_gather | solution.py:40
  121.3 1.4 convolution_convert_fusion
  122.7 1.4 convolution_convert_fusion.1
  124.2 0.7 copy.12
  124.9 0.5 copy-done
  125.4 0.9 fusion.7
  126.3 2.5 %psum.29 = bf16[128]{0:T(256)(128)(2,1)S(1)} all-reduce(bf16[128]{0:T(256)(128)(2,1)S(1)} %convert_element_type.82), channel_id=1, replica_groups=mesh['group'=2,'latent'=8,'dp'=2] {'dp'}, use_global_device_ids=true, to_apply=%region_4.5 | all-reduce | flops 128 | bytes 512 | tf_op jit(solution)/shard_map/psum | solution.py:60
  128.8 57.6 %psum.31 = f32[4096]{0:T(1024)S(1)} all-reduce(f32[4096]{0:T(1024)S(1)} %sub.51), channel_id=1, replica_groups=mesh['group'=2,'latent'=8,'dp'=2] {'latent','dp'}, use_global_device_ids=true, to_apply=%region_7.8 | all-reduce | flops 4096 | bytes 32768 | tf_op jit(solution)/shard_map/psum | solution.py:55
  186.5 0.5 multiply_subtract_fusion.1
  187.0 0.6 multiply_subtract_fusion
  187.6 2.6 %subtract_convert_fusion = bf16[4096,128]{1,0:T(8,128)(2,1)} fusion(bf16[4096,128]{1,0:T(8,128)(2,1)} %get-tuple-element.136, bf16[4096,128]{1,0:T(8,128)(2,1)S(1)} %copy-done), kind=kLoop, calls=%fused_computation.5 | loop fusion | flops 2621440 | bytes 3145728 | tf_op jit(solution)/shard_map/convert_element_type | solution.py:62
  190.6 1.3 copy.13
  (46 shorter events, 2.0 us)
Async XLA Ops:
  7.2 180.4 %all-reduce.3.cloned.1.call-start = ((), (), s32[]{:S(2)}) async-start(), calls=%async_computation | async-start | bytes 4194304 | tf_op jit(solution)/shard_map/psum | solution.py:58
  8.0 34.3 %copy-start.1 = (bf16[128,4096]{1,0:T(8,128)(2,1)S(1)}, bf16[128,4096]{1,0:T(8,128)(2,1)}, u32[]{:S(2)}) copy-start(bf16[128,4096]{1,0:T(8,128)(2,1)} %param.10) | copy-start | bytes 3145732
  42.6 47.3 %copy-start.3 = (bf16[4,4096]{1,0:T(4,128)(2,1)S(1)}, bf16[4,4096]{1,0:T(4,128)(2,1)}, u32[]{:S(2)}) copy-start(bf16[4,4096]{1,0:T(4,128)(2,1)} %param.7) | copy-start | bytes 98308
  42.6 47.3 %copy-start.5 = (f32[4096]{0:T(1024)S(1)}, f32[4096]{0:T(1024)}, u32[]{:S(2)}) copy-start(f32[4096]{0:T(1024)} %param.11) | copy-start | bytes 49156
  42.7 6.7 %collective-permute-start = (bf16[4,4096]{1,0:T(4,128)(2,1)S(1)}, bf16[4,4096]{1,0:T(4,128)(2,1)S(1)}, u32[]{:S(2)}, u32[]{:S(2)}) collective-permute-start(bf16[4,4096]{1,0:T(4,128)(2,1)S(1)} %convert_element_type.126), channel_id=1, source_target_pairs={{14,0},{0,2},{2,4},{4,6},{6,8},{8,10},{10,12},{12,14},{15,1},{1,3}... | collective-permute-start | bytes 98312 | tf_op jit(solution)/shard_map/while/body/eval_jaxpr/ppermute | solution.py:12
  49.4 6.7 %collective-permute-start = (bf16[4,4096]{1,0:T(4,128)(2,1)S(1)}, bf16[4,4096]{1,0:T(4,128)(2,1)S(1)}, u32[]{:S(2)}, u32[]{:S(2)}) collective-permute-start(bf16[4,4096]{1,0:T(4,128)(2,1)S(1)} %convert_element_type.126), channel_id=1, source_target_pairs={{14,0},{0,2},{2,4},{4,6},{6,8},{8,10},{10,12},{12,14},{15,1},{1,3}... | collective-permute-start | bytes 98312 | tf_op jit(solution)/shard_map/while/body/eval_jaxpr/ppermute | solution.py:12
  56.1 6.7 %collective-permute-start = (bf16[4,4096]{1,0:T(4,128)(2,1)S(1)}, bf16[4,4096]{1,0:T(4,128)(2,1)S(1)}, u32[]{:S(2)}, u32[]{:S(2)}) collective-permute-start(bf16[4,4096]{1,0:T(4,128)(2,1)S(1)} %convert_element_type.126), channel_id=1, source_target_pairs={{14,0},{0,2},{2,4},{4,6},{6,8},{8,10},{10,12},{12,14},{15,1},{1,3}... | collective-permute-start | bytes 98312 | tf_op jit(solution)/shard_map/while/body/eval_jaxpr/ppermute | solution.py:12
  62.8 6.7 %collective-permute-start = (bf16[4,4096]{1,0:T(4,128)(2,1)S(1)}, bf16[4,4096]{1,0:T(4,128)(2,1)S(1)}, u32[]{:S(2)}, u32[]{:S(2)}) collective-permute-start(bf16[4,4096]{1,0:T(4,128)(2,1)S(1)} %convert_element_type.126), channel_id=1, source_target_pairs={{14,0},{0,2},{2,4},{4,6},{6,8},{8,10},{10,12},{12,14},{15,1},{1,3}... | collective-permute-start | bytes 98312 | tf_op jit(solution)/shard_map/while/body/eval_jaxpr/ppermute | solution.py:12
  69.6 6.7 %collective-permute-start = (bf16[4,4096]{1,0:T(4,128)(2,1)S(1)}, bf16[4,4096]{1,0:T(4,128)(2,1)S(1)}, u32[]{:S(2)}, u32[]{:S(2)}) collective-permute-start(bf16[4,4096]{1,0:T(4,128)(2,1)S(1)} %convert_element_type.126), channel_id=1, source_target_pairs={{14,0},{0,2},{2,4},{4,6},{6,8},{8,10},{10,12},{12,14},{15,1},{1,3}... | collective-permute-start | bytes 98312 | tf_op jit(solution)/shard_map/while/body/eval_jaxpr/ppermute | solution.py:12
  76.3 6.8 %collective-permute-start = (bf16[4,4096]{1,0:T(4,128)(2,1)S(1)}, bf16[4,4096]{1,0:T(4,128)(2,1)S(1)}, u32[]{:S(2)}, u32[]{:S(2)}) collective-permute-start(bf16[4,4096]{1,0:T(4,128)(2,1)S(1)} %convert_element_type.126), channel_id=1, source_target_pairs={{14,0},{0,2},{2,4},{4,6},{6,8},{8,10},{10,12},{12,14},{15,1},{1,3}... | collective-permute-start | bytes 98312 | tf_op jit(solution)/shard_map/while/body/eval_jaxpr/ppermute | solution.py:12
  83.2 6.7 %collective-permute-start = (bf16[4,4096]{1,0:T(4,128)(2,1)S(1)}, bf16[4,4096]{1,0:T(4,128)(2,1)S(1)}, u32[]{:S(2)}, u32[]{:S(2)}) collective-permute-start(bf16[4,4096]{1,0:T(4,128)(2,1)S(1)} %convert_element_type.126), channel_id=1, source_target_pairs={{14,0},{0,2},{2,4},{4,6},{6,8},{8,10},{10,12},{12,14},{15,1},{1,3}... | collective-permute-start | bytes 98312 | tf_op jit(solution)/shard_map/while/body/eval_jaxpr/ppermute | solution.py:12
  89.9 31.3 %copy-start.4 = (f32[4,4096]{1,0:T(4,128)}, f32[4,4096]{1,0:T(4,128)S(1)}, u32[]{:S(2)}) copy-start(f32[4,4096]{1,0:T(4,128)S(1)} %get-tuple-element.139) | copy-start | bytes 196612
  124.2 1.2 copy-start
  124.9 61.6 %copy-start.6 = (f32[128]{0:T(128)S(1)}, f32[128]{0:T(128)}, u32[]{:S(2)}) copy-start(f32[128]{0:T(128)} %param.9) | copy-start | bytes 1540
  187.6 2.6 %copy-start.2 = (bf16[4096,128]{1,0:T(8,128)(2,1)S(1)}, bf16[4096,128]{1,0:T(8,128)(2,1)}, u32[]{:S(2)}) copy-start(bf16[4096,128]{1,0:T(8,128)(2,1)} %get-tuple-element.137) | copy-start | bytes 3145732
Sparse Core Ops, SparseCore 0:
  124.3 18.5 all-reduce.2
where the time goes:
time: 199 us
  blocking collectives  124 us (62%)
  waiting for transfers between devices  44.6 us (22%)
  between operations  14.2 us (7%)
  matrix products  6.05 us (3%)
  other arithmetic  5.22 us (3%)
  local copies, waits for them, and re-layouts  2.68 us (1%)
  starting transfers between devices  1.99 us (1%)
    psum x1, blocking collectives, on_device(): grad_dec_bias = lax.psum(bias_term, ('latent', 'dp'))  57.6 us
    ppermute x7, waiting for transfers between devices, from_behind(): return lax.ppermute(block, axis, route)  44.6 us
    all_gather x1, blocking collectives, on_device(): gathered = lax.all_gather(centered, 'latent', axis=0, tiled=True)  32.7 us
    all_gather x1, blocking collectives, on_device(): errors = lax.all_gather(recon_error, 'latent', axis=0, tiled=True)  30.7 us
  transfers between devices with their start and end apart: 8, of which 7 were waited for; matrix products, arithmetic and copies ran while one was open for 1% of the time, Pallas kernels for 0%

commit v1 on v0

v1 whole, which is shorter than its diff:
```python
import functools

import jax
import jax.numpy as jnp
from jax import lax
from jax.experimental import pallas as pl
from jax.experimental.pallas import tpu as pltpu
from jax.sharding import PartitionSpec as P

STEP_RATE = 0.1
MESH = pl.DeviceIdType.MESH
ROWS = 16


def kernel(
    nl, factor,
    tokens, enc_hbm, enc_bias, dec_hbm, dec_bias,
    recon_out, new_enc, new_enc_bias, new_dec, new_dec_bias,
    x_all, err_all, r_send, r_recv, enc_cat, dec_cat, e_cat, g_cat, codes_all,
    tok_f, bias_f, work_f, rates, term_send, term_recv, sems, local,
):
    me = lax.axis_index("latent")
    slab = lax.axis_index("dp")
    t, d = tokens.shape
    chunks = ROWS // t
    width = d // chunks
    lat = enc_bias.shape[1]
    nb = 2 * nl
    mine = slab * nl
    other = (1 - slab) * nl

    loads = []
    for c in range(chunks):
        loads.append(pltpu.make_async_copy(
            enc_hbm.at[pl.ds(c * width, width), :], enc_cat.at[:, pl.ds(c * lat, lat)], local.at[0, c]))
    for c in range(chunks):
        loads.append(pltpu.make_async_copy(
            dec_hbm.at[:, pl.ds(c * width, width)], dec_cat.at[pl.ds(c * lat, lat), :], local.at[1, c]))
    for copy in loads:
        copy.start()

    barrier = pltpu.get_barrier_semaphore()

    @pl.loop(1, nl)
    def _(k):
        pl.semaphore_signal(barrier, inc=1, device_id={"latent": lax.rem(me + k, nl)}, device_id_type=MESH)

    pl.semaphore_signal(barrier, inc=1, device_id={"dp": 1 - slab}, device_id_type=MESH)

    for c in range(chunks):
        tok_f[c * t:(c + 1) * t, :] = tokens[:, c * width:(c + 1) * width].astype(jnp.float32)
        bias_f[c * t:(c + 1) * t, :] = jnp.broadcast_to(dec_bias[:, c * width:(c + 1) * width], (t, width))
    x_all[mine + me] = (tok_f[...] - bias_f[...]).astype(jnp.bfloat16)
    pl.semaphore_wait(barrier, nl)

    def to_peer(src, dst, kind, send, recv, peer):
        return pltpu.make_async_remote_copy(
            src_ref=src, dst_ref=dst, send_sem=sems.at[kind, send], recv_sem=sems.at[kind + 1, recv],
            device_id={"latent": peer}, device_id_type=MESH)

    def to_partner(buf, kind, block):
        return pltpu.make_async_remote_copy(
            src_ref=buf.at[mine + block], dst_ref=buf.at[mine + block],
            send_sem=sems.at[kind, block], recv_sem=sems.at[kind + 1, block],
            device_id={"dp": 1 - slab}, device_id_type=MESH)

    def gather_start(buf, kind):
        @pl.loop(1, nl)
        def _(k):
            to_peer(buf.at[mine + me], buf.at[mine + me], kind, k, me, lax.rem(me + k, nl)).start()

        to_partner(buf, kind + 2, me).start()

    def gather_forward(buf, kind):
        @pl.loop(1, nl)
        def _(k):
            src = lax.rem(me + nl - k, nl)
            to_peer(buf.at[mine + src], buf.at[mine + src], kind, k, src, src).wait_recv()
            to_partner(buf, kind + 2, src).start()

    def gather_other(buf, kind):
        @pl.loop(0, nl)
        def _(j):
            pltpu.make_async_remote_copy(
                src_ref=buf.at[other + j], dst_ref=buf.at[other + j],
                send_sem=sems.at[kind + 2, j], recv_sem=sems.at[kind + 3, j],
                device_id={"dp": 1 - slab}, device_id_type=MESH).wait_recv()

    def gather_end(buf, kind):
        @pl.loop(1, nl)
        def _(k):
            to_peer(buf.at[mine + me], buf.at[mine + me], kind, k, me, lax.rem(me + k, nl)).wait_send()

        @pl.loop(0, nl)
        def _(j):
            to_partner(buf, kind + 2, j).wait_send()

    group = 8
    span = group * ROWS
    chunk_of = lax.rem(lax.broadcasted_iota(jnp.int32, (span, lat), 0), ROWS) // t

    def fold(value):
        picked = value[:, :lat]
        for c in range(1, chunks):
            picked = jnp.where(chunk_of == c, value[:, c * lat:(c + 1) * lat], picked)
        picked = picked.reshape(group, ROWS, lat)
        half = picked[:, :8] + picked[:, 8:]
        shift = 4
        while shift >= t:
            half = half + pltpu.roll(half, shift, 1)
            shift //= 2
        return jnp.concatenate([half, half], axis=1).reshape(span, lat)

    def spread(value, dst, row):
        for c in range(chunks):
            dst[pl.ds(row, span), c * lat:(c + 1) * lat] = jnp.where(chunk_of == c, value, 0.0).astype(jnp.bfloat16)

    def encode(first):
        @pl.loop(0, nl // group)
        def _(g):
            block = first + g * group
            row = pl.multiple_of(block * ROWS, span)
            x = x_all[pl.ds(block, group)].reshape(span, width)
            pre = fold(jnp.dot(x, enc_cat[...], preferred_element_type=jnp.float32)) + enc_bias[...]
            codes = jnp.maximum(pre, 0.0).astype(jnp.bfloat16)
            codes_all[pl.ds(row, span), :] = codes
            spread(codes.astype(jnp.float32), e_cat, row)

    gather_start(x_all, 0)
    for c in range(chunks):
        loads[c].wait()
    gather_forward(x_all, 0)
    encode(mine)
    for c in range(chunks):
        loads[chunks + c].wait()

    @pl.loop(0, nl // group)
    def _(g):
        row = pl.multiple_of((mine + g * group) * ROWS, span)
        part = jnp.dot(e_cat[pl.ds(row, span), :], dec_cat[...], preferred_element_type=jnp.float32)
        r_send[pl.ds(g * group, group)] = part.astype(jnp.bfloat16).reshape(group, ROWS, width)

    @pl.loop(1, nl)
    def _(k):
        peer = lax.rem(me + k, nl)
        to_peer(r_send.at[peer], r_recv.at[me], 4, k, me, peer).start()

    gather_other(x_all, 0)
    encode(other)

    work_f[...] = r_send[me].astype(jnp.float32) + bias_f[...]

    @pl.loop(1, nl)
    def _(k):
        src = lax.rem(me + nl - k, nl)
        to_peer(r_send.at[src], r_recv.at[src], 4, k, src, src).wait_recv()
        work_f[...] += r_recv[src].astype(jnp.float32)

    err_all[mine + me] = (work_f[...] - tok_f[...]).astype(jnp.bfloat16)
    gather_start(err_all, 6)
    for c in range(chunks):
        recon_out[:, c * width:(c + 1) * width] = work_f[c * t:(c + 1) * t, :]
    gather_forward(err_all, 6)

    def backward(first, which):
        rates[which:which + 1, :] = jnp.zeros((1, lat), jnp.float32)

        @pl.loop(0, nl // group)
        def _(g):
            block = first + g * group
            row = pl.multiple_of(block * ROWS, span)
            err = err_all[pl.ds(block, group)].reshape(span, width)
            back = fold(lax.dot_general(
                err, dec_cat[...], (((1,), (1,)), ((), ())), preferred_element_type=jnp.float32))
            kept = codes_all[pl.ds(row, span), :].astype(jnp.float32) > 0
            grad = jnp.where(kept, back, 0.0).astype(jnp.bfloat16).astype(jnp.float32)
            spread(grad, g_cat, row)
            rates[which:which + 1, :] += jnp.sum(jnp.where(chunk_of == 0, grad, 0.0), axis=0, keepdims=True)

    backward(mine, 0)
    gather_other(err_all, 6)
    backward(other, 1)

    rate_0, rate_1 = rates[0:1, :], rates[1:2, :]
    new_enc_bias[...] = enc_bias[...] - factor * (
        rate_0.astype(jnp.bfloat16).astype(jnp.float32) + rate_1.astype(jnp.bfloat16).astype(jnp.float32))
    rate = rate_0 + rate_1
    high = rate.astype(jnp.bfloat16).astype(jnp.float32)
    mid = (rate - high).astype(jnp.bfloat16).astype(jnp.float32)
    low = rate - high - mid
    index = lax.broadcasted_iota(jnp.int32, (16, lat), 0)
    pieces = jnp.where(index == 0, high, jnp.where(index == 1, mid, jnp.where(index == 2, low, 0.0)))
    pieces = pieces.astype(jnp.bfloat16)
    eighth = d // 8
    for c in range(chunks):
        term = jnp.sum(lax.dot_general(
            pieces, enc_cat[:, c * lat:(c + 1) * lat], (((1,), (1,)), ((), ())),
            preferred_element_type=jnp.float32), axis=0, keepdims=True)
        for h in range(8 // chunks):
            r = c * (8 // chunks) + h
            term_send[r:r + 1, :] = term[:, h * eighth:(h + 1) * eighth]

    @pl.loop(1, nl)
    def _(k):
        to_peer(term_send, term_recv.at[me], 10, k, me, lax.rem(me + k, nl)).start()

    depth = 256
    tile = 256

    def over_rows(first, second, shape):
        def piece(row):
            return lax.dot_general(
                first(row), second(row), (((0,), (0,)), ((), ())), preferred_element_type=jnp.float32)

        steps = nb * ROWS // depth
        if steps == 1:
            return piece(0)
        return lax.fori_loop(
            0, steps, lambda i, acc: acc + piece(pl.multiple_of(i * depth, depth)), jnp.zeros(shape, jnp.float32))

    def blocks(buf, row, col):
        return buf[pl.ds(row // ROWS, depth // ROWS), :, pl.ds(col, tile)].reshape(depth, tile)

    @pl.loop(0, width // tile)
    def _(i):
        col = pl.multiple_of(i * tile, tile)
        grad = over_rows(
            lambda row: blocks(x_all, row, col), lambda row: g_cat[pl.ds(row, depth), :], (tile, chunks * lat))
        enc_cat[pl.ds(col, tile), :] = (
            enc_cat[pl.ds(col, tile), :].astype(jnp.float32) - factor * grad).astype(jnp.bfloat16)

    stores = []
    for c in range(chunks):
        copy = pltpu.make_async_copy(
            enc_cat.at[:, pl.ds(c * lat, lat)], new_enc.at[pl.ds(c * width, width), :], local.at[2, c])
        copy.start()
        stores.append(copy)

    @pl.loop(0, width // tile)
    def _(i):
        col = pl.multiple_of(i * tile, tile)
        grad = over_rows(
            lambda row: e_cat[pl.ds(row, depth), :], lambda row: blocks(err_all, row, col), (chunks * lat, tile))
        dec_cat[:, pl.ds(col, tile)] = (
            dec_cat[:, pl.ds(col, tile)].astype(jnp.float32) - factor * grad).astype(jnp.bfloat16)

    for c in range(chunks):
        copy = pltpu.make_async_copy(
            dec_cat.at[pl.ds(c * lat, lat), :], new_dec.at[:, pl.ds(c * width, width)], local.at[3, c])
        copy.start()
        stores.append(copy)

    work_f[...] = err_all[0].astype(jnp.float32)

    @pl.loop(1, nb)
    def _(b):
        work_f[...] += err_all[b].astype(jnp.float32)

    total = term_send[...]

    def add_term(k, total):
        src = lax.rem(me + nl - k, nl)
        to_peer(term_send, term_recv.at[src], 10, k, src, src).wait_recv()
        return total + term_recv[src]

    total = lax.fori_loop(1, nl, add_term, total)
    per = 8 // chunks
    for c in range(chunks):
        sums = jnp.sum(work_f[c * t:(c + 1) * t, :], axis=0, keepdims=True)
        for h in range(per):
            r = c * per + h
            cols = slice(r * eighth, (r + 1) * eighth)
            new_dec_bias[:, cols] = dec_bias[:, cols] - factor * (
                sums[:, h * eighth:(h + 1) * eighth] - total[r:r + 1, :])

    gather_end(x_all, 0)
    gather_end(err_all, 6)

    @pl.loop(1, nl)
    def _(k):
        peer = lax.rem(me + k, nl)
        to_peer(r_send.at[peer], r_recv.at[me], 4, k, me, peer).wait_send()
        to_peer(term_send, term_recv.at[me], 10, k, me, peer).wait_send()

    for copy in stores:
        copy.wait()


def on_device(tokens, enc_weight, enc_bias, dec_weight, dec_bias):
    nl = lax.axis_size("latent")
    t, d = tokens.shape
    lat = enc_weight.shape[1]
    nb = 2 * nl
    chunks = ROWS // t
    width = d // chunks
    factor = STEP_RATE * 2.0 / (t * nb)
    vmem = pl.BlockSpec(memory_space=pltpu.VMEM)
    anywhere = pl.BlockSpec(memory_space=pl.ANY)
    bf16, f32 = jnp.bfloat16, jnp.float32
    out = pl.pallas_call(
        functools.partial(kernel, nl, factor),
        out_shape=(
            jax.ShapeDtypeStruct((t, d), f32),
            jax.ShapeDtypeStruct((d, lat), bf16),
            jax.ShapeDtypeStruct((1, lat), f32),
            jax.ShapeDtypeStruct((lat, d), bf16),
            jax.ShapeDtypeStruct((1, d), f32),
        ),
        in_specs=[vmem, anywhere, vmem, anywhere, vmem],
        out_specs=(vmem, anywhere, vmem, anywhere, vmem),
        scratch_shapes=[
            pltpu.VMEM((nb, ROWS, width), bf16),
            pltpu.VMEM((nb, ROWS, width), bf16),
            pltpu.VMEM((nl, ROWS, width), bf16),
            pltpu.VMEM((nl, ROWS, width), bf16),
            pltpu.VMEM((width, chunks * lat), bf16),
            pltpu.VMEM((chunks * lat, width), bf16),
            pltpu.VMEM((nb * ROWS, chunks * lat), bf16),
            pltpu.VMEM((nb * ROWS, chunks * lat), bf16),
            pltpu.VMEM((nb * ROWS, lat), bf16),
            pltpu.VMEM((ROWS, width), f32),
            pltpu.VMEM((ROWS, width), f32),
            pltpu.VMEM((ROWS, width), f32),
            pltpu.VMEM((8, lat), f32),
            pltpu.VMEM((8, d // 8), f32),
            pltpu.VMEM((nl, 8, d // 8), f32),
            pltpu.SemaphoreType.DMA((12, nl)),
            pltpu.SemaphoreType.DMA((4, chunks)),
        ],
        compiler_params=pltpu.CompilerParams(
            collective_id=0, has_side_effects=True, vmem_limit_bytes=56 * 1024 * 1024),
    )(tokens, enc_weight, enc_bias.reshape(1, lat), dec_weight, dec_bias.reshape(1, d))
    recon, new_enc, new_enc_bias, new_dec, new_dec_bias = out
    return recon, new_enc, new_enc_bias.reshape(lat), new_dec, new_dec_bias.reshape(d)


def solution(mesh):
    specs = (
        P(("group", "latent", "dp"), None),
        P("group", "latent"),
        P(("group", "latent")),
        P(("group", "latent"), None),
        P("group"),
    )
    return jax.shard_map(on_device, mesh=mesh, in_specs=specs, out_specs=specs, check_vma=False)
```

time: 199 us -> 43.5 us (0.22)
  blocking collectives: 124 us -> 0 us
  waiting for transfers between devices: 44.6 us -> 0 us
  Pallas kernels: 0 us -> 36.7 us
  between operations: 14.2 us -> 0.65 us
  matrix products: 6.05 us -> 0 us
  other arithmetic: 5.22 us -> 0 us
  local copies, waits for them, and re-layouts: 2.68 us -> 5.92 us
  starting transfers between devices: 1.99 us -> 0 us
    all_gather x2 -> x0, blocking collectives: 63.4 us -> none  [the longest x1 32.7 us: on_device(): gathered = lax.all_gather(centered, 'latent', axis=0, tiled=True)]
    psum x2 -> x0, blocking collectives: 60.1 us -> none  [the longest x1 57.6 us: on_device(): grad_dec_bias = lax.psum(bias_term, ('latent', 'dp'))]
    ppermute x7 -> x0, waiting for transfers between devices: 44.6 us -> none  [from_behind(): return lax.ppermute(block, axis, route)]
    pallas_call x0 -> x1, Pallas kernels: none -> 36.7 us  [on_device(): pl.pallas_call(functools.partial(kernel, nl, factor), out_shape=(jax.Shap...]
    dot_general x6 -> x0, matrix products: 6.05 us -> none  [the longest x1 1.51 us: on_device(): jnp.dot(gathered, enc_weight, preferred_element_type=jnp.float32) + enc_bias]
    unnamed x18 -> x11, local copies, waits for them, and re-layouts: 2.66 us -> 5.92 us
    convert_element_type x10 -> x0, other arithmetic: 3.06 us -> none  [the longest x1 2.62 us: on_device(): (enc_weight.astype(jnp.float32) - factor * summed_enc).astype(jnp.bfloat16)]
  transfers between devices with their start and end apart: 8 -> 0, of which waited for: 7 -> 0; matrix products, arithmetic and copies ran while one was open for 1% -> 0% of each run, Pallas kernels for 0% -> 0%
where the time goes in v1:
time: 43.5 us; the launch traced here: 43.3 us
  Pallas kernels  36.7 us (84%)
  local copies, waits for them, and re-layouts  5.92 us (14%)
  between operations  0.65 us (1%)
    pallas_call x1, Pallas kernels, on_device(): pl.pallas_call(functools.partial(kernel, nl, factor), out_shape=(jax.Shap...  36.7 us
    unnamed x11, local copies, waits for them, and re-layouts  5.92 us

profile of v1, /device:TPU:0, one launch (start us, length us, event | category | flops | bytes accessed | tf_op | source)
XLA Modules:
  0.0 43.3 jit_solution(2454949731281228854)
XLA Ops:
  0.6 36.7 %shard_map.92 = (f32[4,4096]{1,0:T(4,128)}, bf16[4096,128]{1,0:T(8,128)(2,1)}, f32[1,128]{1,0:T(1,128)}, bf16[128,4096]{1,0:T(8,128)(2,1)}, f32[1,4096]{1,0:T(1,128)}) custom-call(bf16[4,4096]{1,0:T(4,128)(2,1)} %tokens.1, bf16[4096,128]{1,0:T(8,128)(2,1)} %enc_hbm.1, f32[1,128]{1,0:T(1,128)} %bitcast.6, bf16[128,4096]{1,0:T(8,128)(2,1)} %dec_hbm.1, ...), custom_call_target="tpu_custom_call" | custom-call | tf_op jit(solution)/shard_map/pallas_call | solution.py:300
  37.3 1.5 %copy.15 = f32[4,4096]{1,0:T(4,128)} copy(f32[4,4096]{1,0:T(4,128)} %get-tuple-element.20) | data formatting | bytes 131072
  38.8 0.0 copy-start.2
  38.8 0.0 copy-start
  38.8 2.4 %copy.16 = bf16[4096,128]{1,0:T(8,128)(2,1)} copy(bf16[4096,128]{1,0:T(8,128)(2,1)} %get-tuple-element.21) | data formatting | bytes 2097152
  41.2 0.0 copy-done.2
  41.2 0.5 %copy.17 = f32[128]{0:T(128)} copy(f32[128]{0:T(128)S(1)} %bitcast.7) | data formatting | bytes 1024
  41.7 0.0 copy-done
  41.7 0.0 copy-start.1
  41.7 1.0 %copy.18 = bf16[128,4096]{1,0:T(8,128)(2,1)} copy(bf16[128,4096]{1,0:T(8,128)(2,1)S(1)} %copy-done) | data formatting | bytes 2097152
  42.7 0.0 copy-done.1
  42.7 0.6 %copy.19 = f32[4096]{0:T(1024)} copy(f32[4096]{0:T(1024)S(1)} %bitcast.5) | data formatting | bytes 32768
Async XLA Ops:
  38.8 2.4 %copy-start.2 = (f32[1,128]{1,0:T(1,128)S(1)}, f32[1,128]{1,0:T(1,128)}, u32[]{:S(2)}) copy-start(f32[1,128]{1,0:T(1,128)} %get-tuple-element.12) | copy-start | bytes 1540
  38.8 2.9 %copy-start = (bf16[128,4096]{1,0:T(8,128)(2,1)S(1)}, bf16[128,4096]{1,0:T(8,128)(2,1)}, u32[]{:S(2)}) copy-start(bf16[128,4096]{1,0:T(8,128)(2,1)} %get-tuple-element.23) | copy-start | bytes 3145732
  41.7 1.0 %copy-start.1 = (f32[1,4096]{1,0:T(1,128)S(1)}, f32[1,4096]{1,0:T(1,128)}, u32[]{:S(2)}) copy-start(f32[1,4096]{1,0:T(1,128)} %get-tuple-element.14) | copy-start | bytes 49156

commit v2 on v1

--- a/solution.py
+++ b/solution.py
@@ -14,10 +14,10 @@
 
 def kernel(
     nl, factor,
-    tokens, enc_hbm, enc_bias, dec_hbm, dec_bias,
+    tokens_hbm, enc_hbm, enc_bias_hbm, dec_hbm, dec_bias_hbm,
     recon_out, new_enc, new_enc_bias, new_dec, new_dec_bias,
     x_all, err_all, r_send, r_recv, enc_cat, dec_cat, e_cat, g_cat, codes_all,
-    tok_f, bias_f, work_f, rates, term_send, term_recv, sems, local,
+    tok_f, bias_f, work_f, rates, term_send, term_recv, tokens, enc_bias, dec_bias, sems, local, small,
 ):
     me = lax.axis_index("latent")
     slab = lax.axis_index("dp")
@@ -29,6 +29,11 @@
     mine = slab * nl
     other = (1 - slab) * nl
 
+    first_loads = [
+        pltpu.make_async_copy(src, dst, small.at[i])
+        for i, (src, dst) in enumerate(((tokens_hbm, tokens), (dec_bias_hbm, dec_bias), (enc_bias_hbm, enc_bias)))]
+    for copy in first_loads:
+        copy.start()
     loads = []
     for c in range(chunks):
         loads.append(pltpu.make_async_copy(
@@ -47,6 +52,8 @@
 
     pl.semaphore_signal(barrier, inc=1, device_id={"dp": 1 - slab}, device_id_type=MESH)
 
+    for copy in first_loads:
+        copy.wait()
     for c in range(chunks):
         tok_f[c * t:(c + 1) * t, :] = tokens[:, c * width:(c + 1) * width].astype(jnp.float32)
         bias_f[c * t:(c + 1) * t, :] = jnp.broadcast_to(dec_bias[:, c * width:(c + 1) * width], (t, width))
@@ -64,18 +71,31 @@
             send_sem=sems.at[kind, block], recv_sem=sems.at[kind + 1, block],
             device_id={"dp": 1 - slab}, device_id_type=MESH)
 
+    pair = me + 1 - 2 * lax.rem(me, 2)
+
     def gather_start(buf, kind):
-        @pl.loop(1, nl)
+        @pl.loop(1, nl // 2)
         def _(k):
-            to_peer(buf.at[mine + me], buf.at[mine + me], kind, k, me, lax.rem(me + k, nl)).start()
-
+            to_peer(buf.at[mine + me], buf.at[mine + me], kind, k, me, lax.rem(me + 2 * k, nl)).start()
+
+        to_peer(buf.at[mine + me], buf.at[mine + me], kind, 0, me, pair).start()
         to_partner(buf, kind + 2, me).start()
 
     def gather_forward(buf, kind):
-        @pl.loop(1, nl)
+        def arrived(src):
+            to_peer(buf.at[mine + src], buf.at[mine + src], kind, 0, src, src).wait_recv()
+
+        @pl.loop(1, nl // 2)
         def _(k):
-            src = lax.rem(me + nl - k, nl)
-            to_peer(buf.at[mine + src], buf.at[mine + src], kind, k, src, src).wait_recv()
+            src = lax.rem(me + nl - 2 * k, nl)
+            arrived(src)
+            to_peer(buf.at[mine + src], buf.at[mine + src], kind, nl // 2 + k, src, pair).start()
+            to_partner(buf, kind + 2, src).start()
+
+        @pl.loop(0, nl // 2)
+        def _(k):
+            src = lax.rem(pair + nl - 2 * k, nl)
+            arrived(src)
             to_partner(buf, kind + 2, src).start()
 
     def gather_other(buf, kind):
@@ -87,9 +107,12 @@
                 device_id={"dp": 1 - slab}, device_id_type=MESH).wait_recv()
 
     def gather_end(buf, kind):
-        @pl.loop(1, nl)
+        @pl.loop(1, nl // 2)
         def _(k):
-            to_peer(buf.at[mine + me], buf.at[mine + me], kind, k, me, lax.rem(me + k, nl)).wait_send()
+            to_peer(buf.at[mine + me], buf.at[mine + me], kind, k, me, pair).wait_send()
+            to_peer(buf.at[mine + me], buf.at[mine + me], kind, nl // 2 + k, me, pair).wait_send()
+
+        to_peer(buf.at[mine + me], buf.at[mine + me], kind, 0, me, pair).wait_send()
 
         @pl.loop(0, nl)
         def _(j):
@@ -286,6 +309,27 @@
         copy.wait()
 
 
+def hand_on(*refs):
+    count = (len(refs) - 1) // 3
+    sems = refs[-1]
+    loads, stores = [], []
+    for i in range(count):
+        src, dst, held = refs[i], refs[count + i], refs[2 * count + i]
+        rows = src.shape[0]
+        cuts = 4 if rows % 64 == 0 else 1
+        for c in range(cuts):
+            part = pl.ds(c * (rows // cuts), rows // cuts)
+            loads.append(pltpu.make_async_copy(src.at[part], held.at[part], sems.at[0, i, c]))
+            stores.append(pltpu.make_async_copy(held.at[part], dst.at[part], sems.at[1, i, c]))
+    for load in loads:
+        load.start()
+    for load, store in zip(loads, stores):
+        load.wait()
+        store.start()
+    for store in stores:
+        store.wait()
+
+
 def on_device(tokens, enc_weight, enc_bias, dec_weight, dec_bias):
     nl = lax.axis_size("latent")
     t, d = tokens.shape
@@ -294,6 +338,7 @@
     chunks = ROWS // t
     width = d // chunks
     factor = STEP_RATE * 2.0 / (t * nb)
+    scratch_bytes = (6 * nl + 2 * nb + 2 * ROWS) * ROWS * width * 2 + 4 * nb * ROWS * chunks * lat * 2 + nl * d * 4
     vmem = pl.BlockSpec(memory_space=pltpu.VMEM)
     anywhere = pl.BlockSpec(memory_space=pl.ANY)
     bf16, f32 = jnp.bfloat16, jnp.float32
@@ -306,7 +351,7 @@
             jax.ShapeDtypeStruct((lat, d), bf16),
             jax.ShapeDtypeStruct((1, d), f32),
         ),
-        in_specs=[vmem, anywhere, vmem, anywhere, vmem],
+        in_specs=[pl.BlockSpec(memory_space=pltpu.HBM)] * 5,
         out_specs=(vmem, anywhere, vmem, anywhere, vmem),
         scratch_shapes=[
             pltpu.VMEM((nb, ROWS, width), bf16),
@@ -324,12 +369,24 @@
             pltpu.VMEM((8, lat), f32),
             pltpu.VMEM((8, d // 8), f32),
             pltpu.VMEM((nl, 8, d // 8), f32),
+            pltpu.VMEM((t, d), bf16),
+            pltpu.VMEM((1, lat), f32),
+            pltpu.VMEM((1, d), f32),
             pltpu.SemaphoreType.DMA((12, nl)),
             pltpu.SemaphoreType.DMA((4, chunks)),
+            pltpu.SemaphoreType.DMA((3,)),
         ],
         compiler_params=pltpu.CompilerParams(
-            collective_id=0, has_side_effects=True, vmem_limit_bytes=56 * 1024 * 1024),
+            collective_id=0, has_side_effects=True, vmem_limit_bytes=60 * 1024 * 1024),
     )(tokens, enc_weight, enc_bias.reshape(1, lat), dec_weight, dec_bias.reshape(1, d))
+    out = pl.pallas_call(
+        hand_on,
+        out_shape=tuple(jax.ShapeDtypeStruct(o.shape, o.dtype) for o in out),
+        in_specs=[anywhere] * len(out),
+        out_specs=(anywhere,) * len(out),
+        scratch_shapes=[pltpu.VMEM(o.shape, o.dtype) for o in out] + [pltpu.SemaphoreType.DMA((2, len(out), 4))],
+        compiler_params=pltpu.CompilerParams(vmem_limit_bytes=60 * 1024 * 1024),
+    )(*out)
     recon, new_enc, new_enc_bias, new_dec, new_dec_bias = out
     return recon, new_enc, new_enc_bias.reshape(lat), new_dec, new_dec_bias.reshape(d)
 

time: 43.5 us -> 39.3 us (0.903)
  local copies, waits for them, and re-layouts: 5.92 us -> 0 us
  Pallas kernels: 36.7 us -> 38.5 us
    unnamed x11 -> x0, local copies, waits for them, and re-layouts: 5.92 us -> none
    pallas_call x0 -> x1, Pallas kernels: none -> 2.66 us  [on_device(): pl.pallas_call(hand_on, out_shape=tuple((jax.ShapeDtypeStruct(o.shape, o....]
    pallas_call x1, Pallas kernels: 36.7 us -> 35.9 us  [on_device(): pl.pallas_call(functools.partial(kernel, nl, factor), out_shape=(jax.Shap...]
where the time goes in v2:
time: 39.3 us; the launch traced here: 39.2 us
  Pallas kernels  38.5 us (98%)
  between operations  0.64 us (2%)
    pallas_call x1, Pallas kernels, on_device(): pl.pallas_call(functools.partial(kernel, nl, factor), out_shape=(jax.Shap...  35.9 us
    pallas_call x1, Pallas kernels, on_device(): pl.pallas_call(hand_on, out_shape=tuple((jax.ShapeDtypeStruct(o.shape, o....  2.66 us

profile of v2, /device:TPU:0, one launch (start us, length us, event | category | flops | bytes accessed | tf_op | source)
XLA Modules:
  0.0 39.2 jit_solution(8928841349913917776)
XLA Ops:
  0.6 35.9 %shard_map.92 = (f32[4,4096]{1,0:T(4,128)}, bf16[4096,128]{1,0:T(8,128)(2,1)}, f32[1,128]{1,0:T(1,128)}, bf16[128,4096]{1,0:T(8,128)(2,1)}, f32[1,4096]{1,0:T(1,128)}) custom-call(bf16[4,4096]{1,0:T(4,128)(2,1)} %tokens_hbm.1, bf16[4096,128]{1,0:T(8,128)(2,1)} %enc_hbm.1, f32[1,128]{1,0:T(1,128)} %bitcast.5, bf16[128,4096]{1,0:T(8,128)(2,1)} %dec_hbm.1, ...), custom_call_target="tpu_custom_call" | custom-call | tf_op jit(solution)/shard_map/pallas_call | solution.py:345
  36.5 2.7 %shard_map.93 = (f32[4,4096]{1,0:T(4,128)}, bf16[4096,128]{1,0:T(8,128)(2,1)}, f32[1,128]{1,0:T(1,128)}, bf16[128,4096]{1,0:T(8,128)(2,1)}, f32[1,4096]{1,0:T(1,128)}) custom-call(f32[4,4096]{1,0:T(4,128)} %get-tuple-element.15.refs_0_, bf16[4096,128]{1,0:T(8,128)(2,1)} %get-tuple-element.16.refs_1_, f32[1,128]{1,0:T(1,128)} %get-tuple-element.17.refs_2_, ...), custom_call_target="tpu_custom_call" | custom-call | tf_op jit(solution)/shard_map/pallas_call | solution.py:382

commit v3 on v2

--- a/solution.py
+++ b/solution.py
@@ -29,6 +29,14 @@
     mine = slab * nl
     other = (1 - slab) * nl
 
+    barrier = pltpu.get_barrier_semaphore()
+
+    @pl.loop(1, nl)
+    def _(k):
+        pl.semaphore_signal(barrier, inc=1, device_id={"latent": lax.rem(me + k, nl)}, device_id_type=MESH)
+
+    pl.semaphore_signal(barrier, inc=1, device_id={"dp": 1 - slab}, device_id_type=MESH)
+
     first_loads = [
         pltpu.make_async_copy(src, dst, small.at[i])
         for i, (src, dst) in enumerate(((tokens_hbm, tokens), (dec_bias_hbm, dec_bias), (enc_bias_hbm, enc_bias)))]
@@ -44,14 +52,6 @@
     for copy in loads:
         copy.start()
 
-    barrier = pltpu.get_barrier_semaphore()
-
-    @pl.loop(1, nl)
-    def _(k):
-        pl.semaphore_signal(barrier, inc=1, device_id={"latent": lax.rem(me + k, nl)}, device_id_type=MESH)
-
-    pl.semaphore_signal(barrier, inc=1, device_id={"dp": 1 - slab}, device_id_type=MESH)
-
     for copy in first_loads:
         copy.wait()
     for c in range(chunks):
@@ -74,11 +74,12 @@
     pair = me + 1 - 2 * lax.rem(me, 2)
 
     def gather_start(buf, kind):
+        to_peer(buf.at[mine + me], buf.at[mine + me], kind, 0, me, pair).start()
+
         @pl.loop(1, nl // 2)
         def _(k):
             to_peer(buf.at[mine + me], buf.at[mine + me], kind, k, me, lax.rem(me + 2 * k, nl)).start()
 
-        to_peer(buf.at[mine + me], buf.at[mine + me], kind, 0, me, pair).start()
         to_partner(buf, kind + 2, me).start()
 
     def gather_forward(buf, kind):

time: 39.3 us -> 39.3 us (level)
  no operation moved by 1% of the time
where the time goes in v3:
time: 39.3 us; the launch traced here: 39.1 us
  Pallas kernels  38.5 us (98%)
  between operations  0.64 us (2%)
    pallas_call x1, Pallas kernels, on_device(): pl.pallas_call(functools.partial(kernel, nl, factor), out_shape=(jax.Shap...  35.8 us
    pallas_call x1, Pallas kernels, on_device(): pl.pallas_call(hand_on, out_shape=tuple((jax.ShapeDtypeStruct(o.shape, o....  2.66 us

profile of v3, /device:TPU:0, one launch (start us, length us, event | category | flops | bytes accessed | tf_op | source)
XLA Modules:
  0.0 39.1 jit_solution(7636923724058821858)
XLA Ops:
  0.6 35.8 %shard_map.92 = (f32[4,4096]{1,0:T(4,128)}, bf16[4096,128]{1,0:T(8,128)(2,1)}, f32[1,128]{1,0:T(1,128)}, bf16[128,4096]{1,0:T(8,128)(2,1)}, f32[1,4096]{1,0:T(1,128)}) custom-call(bf16[4,4096]{1,0:T(4,128)(2,1)} %tokens_hbm.1, bf16[4096,128]{1,0:T(8,128)(2,1)} %enc_hbm.1, f32[1,128]{1,0:T(1,128)} %bitcast.5, bf16[128,4096]{1,0:T(8,128)(2,1)} %dec_hbm.1, ...), custom_call_target="tpu_custom_call" | custom-call | tf_op jit(solution)/shard_map/pallas_call | solution.py:346
  36.4 2.7 %shard_map.93 = (f32[4,4096]{1,0:T(4,128)}, bf16[4096,128]{1,0:T(8,128)(2,1)}, f32[1,128]{1,0:T(1,128)}, bf16[128,4096]{1,0:T(8,128)(2,1)}, f32[1,4096]{1,0:T(1,128)}) custom-call(f32[4,4096]{1,0:T(4,128)} %get-tuple-element.15.refs_0_, bf16[4096,128]{1,0:T(8,128)(2,1)} %get-tuple-element.16.refs_1_, f32[1,128]{1,0:T(1,128)} %get-tuple-element.17.refs_2_, ...), custom_call_target="tpu_custom_call" | custom-call | tf_op jit(solution)/shard_map/pallas_call | solution.py:383
